TPU v7x, 32 devices: a whole 2x2x4 slice. The times are simulated.
32 devices in a mesh: ctx: 16 (over z, x, core), head: 2 (over y).
Axes of the slice: x: 2, y: 2, z: 4, core: 2. Of those that a mesh axis runs over, the one named last changes fastest.
Arguments:
- queries: bfloat16 [8192, 16, 128], P('ctx', 'head'), may hold values from -40 to 40
- keys: bfloat16 [8192, 128], P('ctx'), may hold values from -5 to 5
- values: bfloat16 [8192, 128], P('ctx'), may hold values from -1.5 to 1.5
- grad_out: bfloat16 [8192, 16, 128], P('ctx', 'head'), may hold values from -6 to 6
- lengths: int32 [16], replicated, may hold values from 1 to 1024, 8192 in all
- tile_of: int32 [16], replicated, may hold values from 0 to 15, each once
Outputs:
- attended: bfloat16 [8192, 16, 128], P('ctx', 'head')
- grad_queries: bfloat16 [8192, 16, 128], P('ctx', 'head')
- grad_keys: float32 [8192, 128], P('ctx')
- grad_values: float32 [8192, 128], P('ctx')
Inputs may be any that keep to these rules, and one draw needn't show every extreme that they name: 16 positive lengths summing to 8192; the longest is exactly 1024. `tile_of`: each tile number appears once.
All inputs are finite; a program needn't handle non-finite values.
Results may differ from a plain program's by a relative error of at most 0.025.
Values may be sent and summed in bfloat16 or wider, within the bound.
No kernel may reach another device: no remote copies, remote signals or barrier semaphores. Data moves between devices by JAX's collectives and lax.ppermute only.
A program may use at most 128 MiB of HBM per device.

v0:
```python
import functools

import jax
import jax.numpy as jnp
from jax import lax
from jax.experimental import pallas as pl
from jax.experimental.pallas import tpu as pltpu
from jax.sharding import PartitionSpec as P

LOG2E = 1.4426950408889634
NEG_FILL = -1e30
KEY_BLOCK = 256
ROW_BLOCK = 512
VMEM_LIMIT = 48 * 1024 * 1024
SMEM = pl.BlockSpec(memory_space=pltpu.SMEM)
F32 = jnp.float32
BF16 = jnp.bfloat16


def matmul(left, right):
    return lax.dot_general(left, right, (((1,), (0,)), ((), ())), preferred_element_type=F32)


def fold_rows(block, combine):
    folded = block[0:8]
    for begin in range(8, block.shape[0], 8):
        folded = combine(folded, block[begin : begin + 8])
    return folded


def block_rows(block):
    return pl.ds(pl.multiple_of(block * KEY_BLOCK, KEY_BLOCK), KEY_BLOCK)


class Spans:
    def __init__(self, heads, tile_rows, place_ref, lengths_ref, tile_of_ref, back):
        chunk = pl.program_id(0)
        chunk_pos = ROW_BLOCK // heads
        self.my_tile = tile_of_ref[place_ref[0]]
        self.base = (self.my_tile - back) * tile_rows
        self.first_pos = self.my_tile * tile_rows + chunk * chunk_pos
        self.ends = []
        total = jnp.int32(0)
        for doc in range(lengths_ref.shape[0]):
            total = total + lengths_ref[doc]
            self.ends.append(total)
        first_start = jnp.int32(0)
        for end in self.ends:
            first_start = jnp.where(end <= self.first_pos, end, first_start)
        self.first_block = lax.div(jnp.maximum(first_start - self.base, 0), KEY_BLOCK)
        reach = self.first_pos + chunk_pos - 1 - self.base
        self.last_block = lax.div(reach, KEY_BLOCK) + 1
        self.heads = heads

    def limits(self):
        lane = lax.broadcasted_iota(jnp.int32, (1, ROW_BLOCK), 1)
        q_pos = self.first_pos + lax.div(lane, self.heads)
        start = jnp.zeros((1, ROW_BLOCK), jnp.int32)
        for end in self.ends:
            start = jnp.where(end <= q_pos, end, start)
        return start - self.base, q_pos - self.base


def key_positions(block):
    return block * KEY_BLOCK + lax.broadcasted_iota(jnp.int32, (KEY_BLOCK, ROW_BLOCK), 0)


def own_forward_kernel(
    heads,
    place_ref,
    lengths_ref,
    tile_of_ref,
    q_ref,
    g_ref,
    k_ref,
    v_ref,
    q_turned_ref,
    g_turned_ref,
    weight_ref,
    out_ref,
    stats_ref,
    v_turned,
    score_buf,
):
    tile_rows, width = k_ref.shape
    exponent_scale = float(width) ** (-0.5) * LOG2E
    spans = Spans(heads, tile_rows, place_ref, lengths_ref, tile_of_ref, 0)

    @pl.when(pl.program_id(0) == 0)
    def turn_values():
        v_turned[...] = v_ref[...].T

    q_turned = q_ref[...].T
    q_turned_ref[...] = q_turned
    g_turned_ref[...] = g_ref[...].T
    low, high = spans.limits()

    def score_step(block, top):
        keys = block_rows(block)
        score = matmul(k_ref[keys, :], q_turned)
        key_pos = key_positions(block)
        score = jnp.where((key_pos >= low) & (key_pos <= high), score, NEG_FILL)
        score_buf[keys, :] = score
        return jnp.maximum(top, fold_rows(score, jnp.maximum))

    top = lax.fori_loop(
        spans.first_block,
        spans.last_block,
        score_step,
        jnp.full((8, ROW_BLOCK), NEG_FILL, F32),
    )
    top = jnp.max(top, axis=0, keepdims=True) * exponent_scale

    def weight_step(block, carried):
        sums, out_turned = carried
        keys = block_rows(block)
        weight = jnp.exp2(score_buf[keys, :] * exponent_scale - top)
        weight_low = weight.astype(BF16)
        weight_ref[keys, :] = weight_low
        out_turned = out_turned + matmul(v_turned[:, keys], weight_low)
        return sums + fold_rows(weight, jnp.add), out_turned

    sums, out_turned = lax.fori_loop(
        spans.first_block,
        spans.last_block,
        weight_step,
        (jnp.zeros((8, ROW_BLOCK), F32), jnp.zeros((width, ROW_BLOCK), F32)),
    )
    out_ref[...] = out_turned
    stats_ref[0:1, :] = top
    stats_ref[1:2, :] = jnp.sum(sums, axis=0, keepdims=True)


def unpack(window, tile_rows, pieces_ref, store):
    n_all, _, piece, _ = pieces_ref.shape
    for slot in range(window):
        for owner in range(n_all):
            begin = slot * tile_rows + owner * piece
            store(begin, piece, pieces_ref[owner, slot])


def pack(window, tile_rows, pieces_ref, load):
    n_all, _, piece, _ = pieces_ref.shape
    for slot in range(window):
        for owner in range(n_all):
            begin = slot * tile_rows + owner * piece
            pieces_ref[owner, slot] = load(begin, piece)


def past_weights_kernel(
    window,
    heads,
    tile_rows,
    place_ref,
    lengths_ref,
    tile_of_ref,
    q_turned_ref,
    g_ref,
    own_stats_ref,
    past_keys_ref,
    prob_ref,
    stats_ref,
    dv_ref,
    k_win,
    score_buf,
    dv_acc,
):
    width = k_win.shape[1]
    past_blocks = window * tile_rows // KEY_BLOCK
    exponent_scale = float(width) ** (-0.5) * LOG2E
    spans = Spans(heads, tile_rows, place_ref, lengths_ref, tile_of_ref, window)
    first_block = spans.first_block

    @pl.when(pl.program_id(0) == 0)
    def begin():
        def store(begin_row, size, rows):
            k_win[begin_row : begin_row + size, :] = rows

        unpack(window, tile_rows, past_keys_ref, store)
        dv_acc[...] = jnp.zeros_like(dv_acc)

    q_turned = q_turned_ref[...]
    g_rows = g_ref[...]
    low, _ = spans.limits()

    def score_step(block, top):
        keys = block_rows(block)
        score = matmul(k_win[keys, :], q_turned)
        score = jnp.where(key_positions(block) >= low, score, NEG_FILL)
        score_buf[keys, :] = score
        return jnp.maximum(top, fold_rows(score, jnp.maximum))

    past_top = lax.fori_loop(
        first_block, past_blocks, score_step, jnp.full((8, ROW_BLOCK), NEG_FILL, F32)
    )
    past_top = jnp.max(past_top, axis=0, keepdims=True) * exponent_scale
    own_top = own_stats_ref[0:1, :]
    top = jnp.maximum(own_top, past_top)

    def weight_step(block, sums):
        keys = block_rows(block)
        weight = jnp.exp2(score_buf[keys, :] * exponent_scale - top)
        score_buf[keys, :] = weight
        return sums + fold_rows(weight, jnp.add)

    sums = lax.fori_loop(
        first_block, past_blocks, weight_step, jnp.zeros((8, ROW_BLOCK), F32)
    )
    rescale = jnp.exp2(own_top - top)
    inverse = 1.0 / (
        own_stats_ref[1:2, :] * rescale + jnp.sum(sums, axis=0, keepdims=True)
    )
    stats_ref[0:1, :] = rescale * inverse

    def value_step(block, carry):
        keys = block_rows(block)
        prob = (score_buf[keys, :] * inverse).astype(BF16)
        prob_ref[keys, :] = prob
        dv_acc[keys, :] += matmul(prob, g_rows)
        return carry

    lax.fori_loop(first_block, past_blocks, value_step, 0)

    @pl.when(pl.program_id(0) == pl.num_programs(0) - 1)
    def finish():
        pack(
            window,
            tile_rows,
            dv_ref,
            lambda begin_row, size: dv_acc[begin_row : begin_row + size, :].astype(BF16),
        )


def past_grads_kernel(
    window,
    heads,
    tile_rows,
    place_ref,
    lengths_ref,
    tile_of_ref,
    q_ref,
    g_turned_ref,
    prob_ref,
    stats_ref,
    own_out_ref,
    past_keys_ref,
    past_values_ref,
    att_ref,
    delta_ref,
    dq_ref,
    dk_ref,
    k_win,
    v_win,
    k_turned,
    v_turned,
    dk_acc,
):
    width = k_win.shape[1]
    past_blocks = window * tile_rows // KEY_BLOCK
    scale = float(width) ** (-0.5)
    spans = Spans(heads, tile_rows, place_ref, lengths_ref, tile_of_ref, window)
    first_block = spans.first_block

    @pl.when(pl.program_id(0) == 0)
    def begin():
        def store_keys(begin_row, size, rows):
            k_win[begin_row : begin_row + size, :] = rows

        def store_values(begin_row, size, rows):
            v_win[begin_row : begin_row + size, :] = rows

        unpack(window, tile_rows, past_keys_ref, store_keys)
        unpack(window, tile_rows, past_values_ref, store_values)
        k_turned[...] = k_win[...].T
        v_turned[...] = v_win[...].T
        dk_acc[...] = jnp.zeros_like(dk_acc)

    q_rows = q_ref[...]
    g_turned = g_turned_ref[...]

    def attend_step(block, out_turned):
        keys = block_rows(block)
        return out_turned + matmul(v_turned[:, keys], prob_ref[keys, :])

    out_turned = lax.fori_loop(
        first_block, past_blocks, attend_step, own_out_ref[...] * stats_ref[0:1, :]
    )
    att_ref[...] = out_turned.T.astype(BF16)
    delta = jnp.sum(out_turned * g_turned.astype(F32), axis=0, keepdims=True)
    delta_ref[0:1, :] = delta

    def grad_step(block, dq_turned):
        keys = block_rows(block)
        dprob = matmul(v_win[keys, :], g_turned)
        dscore = (prob_ref[keys, :].astype(F32) * (dprob - delta)).astype(BF16)
        dk_acc[keys, :] += matmul(dscore, q_rows)
        return dq_turned + matmul(k_turned[:, keys], dscore)

    dq_ref[...] = lax.fori_loop(
        first_block, past_blocks, grad_step, jnp.zeros((width, ROW_BLOCK), F32)
    )

    @pl.when(pl.program_id(0) == pl.num_programs(0) - 1)
    def finish():
        pack(
            window,
            tile_rows,
            dk_ref,
            lambda begin_row, size: (
                dk_acc[begin_row : begin_row + size, :] * scale
            ).astype(BF16),
        )


def own_grads_kernel(
    heads,
    place_ref,
    lengths_ref,
    tile_of_ref,
    q_ref,
    g_ref,
    g_turned_ref,
    weight_ref,
    stats_ref,
    delta_ref,
    past_dq_ref,
    k_ref,
    v_ref,
    dq_ref,
    dkv_ref,
    k_turned,
    dk_acc,
    dv_acc,
):
    tile_rows, width = k_ref.shape
    scale = float(width) ** (-0.5)
    spans = Spans(heads, tile_rows, place_ref, lengths_ref, tile_of_ref, 0)

    @pl.when(pl.program_id(0) == 0)
    def begin():
        k_turned[...] = k_ref[...].T
        dk_acc[...] = jnp.zeros_like(dk_acc)
        dv_acc[...] = jnp.zeros_like(dv_acc)

    q_rows = q_ref[...]
    g_rows = g_ref[...]
    g_turned = g_turned_ref[...]
    rescale = stats_ref[0:1, :]
    delta = delta_ref[0:1, :]

    def grad_step(block, dq_turned):
        keys = block_rows(block)
        prob = weight_ref[keys, :].astype(F32) * rescale
        dprob = matmul(v_ref[keys, :], g_turned)
        dscore = (prob * (dprob - delta)).astype(BF16)
        dv_acc[keys, :] += matmul(prob.astype(BF16), g_rows)
        dk_acc[keys, :] += matmul(dscore, q_rows)
        return dq_turned + matmul(k_turned[:, keys], dscore)

    dq_turned = lax.fori_loop(
        spans.first_block, spans.last_block, grad_step, past_dq_ref[...]
    )
    dq_ref[...] = (dq_turned * scale).T.astype(BF16)

    @pl.when(pl.program_id(0) == pl.num_programs(0) - 1)
    def finish():
        dkv_ref[0] = (dk_acc[...] * scale).astype(BF16)
        dkv_ref[1] = dv_acc[...].astype(BF16)


def route_kernel(window, tile_of_ref, held_ref, out_ref, holder):
    n_ctx, n_head = out_ref.shape[:2]
    for ctx in range(n_ctx):
        holder[tile_of_ref[ctx]] = ctx

    def one(ctx, carry):
        for slot in range(window):
            tile = tile_of_ref[ctx] - (window - slot)
            source = holder[jnp.maximum(tile, 0)]
            rows = held_ref[source]
            for head in range(n_head):
                out_ref[ctx, head, slot] = rows
        return carry

    lax.fori_loop(0, n_ctx, one, 0)


def sum_kernel(window, tile_of_ref, terms_ref, out_ref, holder):
    n_ctx, n_head = out_ref.shape[:2]
    for ctx in range(n_ctx):
        holder[tile_of_ref[ctx]] = ctx

    def one(ctx, carry):
        total = jnp.zeros(out_ref.shape[2:], F32)
        for slot in range(window):
            tile = tile_of_ref[ctx] + (window - slot)
            source = holder[jnp.minimum(tile, n_ctx - 1)]
            part = terms_ref[source, 0, slot].astype(F32)
            for head in range(1, n_head):
                part = part + terms_ref[source, head, slot].astype(F32)
            total = total + jnp.where(tile < n_ctx, part, 0.0)
        for head in range(n_head):
            out_ref[ctx, head] = total.astype(BF16)
        return carry

    lax.fori_loop(0, n_ctx, one, 0)


def whole(shape):
    return pl.BlockSpec(shape, lambda chunk: (0,) * len(shape))


def rows_of(width):
    return pl.BlockSpec((ROW_BLOCK, width), lambda chunk: (chunk, 0))


def columns_of(height):
    return pl.BlockSpec((height, ROW_BLOCK), lambda chunk: (0, chunk))


def shape_of(shape, dtype):
    return jax.ShapeDtypeStruct(shape, dtype)


def chunked_call(body, name, row_total, in_specs, out_specs, out_shape, scratch, flops):
    return pl.pallas_call(
        body,
        grid=(row_total // ROW_BLOCK,),
        in_specs=[SMEM] * 3 + in_specs,
        out_specs=out_specs,
        out_shape=out_shape,
        scratch_shapes=scratch,
        compiler_params=pltpu.CompilerParams(vmem_limit_bytes=VMEM_LIMIT),
        cost_estimate=pl.CostEstimate(
            flops=flops, bytes_accessed=1 << 22, transcendentals=0
        ),
        name=name,
    )


def small_call(body, name, out_shape, n_ctx):
    vmem = pl.BlockSpec(memory_space=pltpu.VMEM)
    return pl.pallas_call(
        body,
        in_specs=[SMEM, vmem],
        out_specs=vmem,
        out_shape=out_shape,
        scratch_shapes=[pltpu.SMEM((n_ctx,), jnp.int32)],
        name=name,
    )


def on_device(queries, keys, values, grad_out, lengths, tile_of):
    tile_rows, heads, width = queries.shape
    n_ctx = lax.axis_size("ctx")
    n_head = lax.axis_size("head")
    n_all = n_ctx * n_head
    piece = tile_rows // n_all
    both = ("ctx", "head")
    most_doc = n_ctx * tile_rows // 8
    window = -(-(most_doc - 1) // tile_rows)
    past_rows = window * tile_rows
    row_total = tile_rows * heads
    place = lax.axis_index("ctx").astype(jnp.int32).reshape(1)
    y = lax.axis_index("head")
    scalars = (place, lengths, tile_of)
    q_rows = queries.reshape(row_total, width)
    g_rows = grad_out.reshape(row_total, width)
    work = 2 * row_total * tile_rows * width
    fine = piece % 16 == 0

    def spread(tile):
        pieces = tile.reshape(n_ctx, n_head, piece, width)
        mine = lax.dynamic_index_in_dim(pieces, y, 1, keepdims=False)
        return lax.all_to_all(mine, "ctx", 0, 0, tiled=True)

    def fetch(held):
        packed = small_call(
            functools.partial(route_kernel, window),
            "route",
            shape_of((n_ctx, n_head, window, piece, width), BF16),
            n_ctx,
        )(tile_of, held)
        past = lax.all_to_all(
            packed.reshape(n_all, window, piece, width), both, 0, 0, tiled=True
        )
        if not fine:
            past = past.transpose(1, 0, 2, 3).reshape(1, window, tile_rows, width)
        return past

    pieces_shape = (n_all, window, piece, width) if fine else (1, window, tile_rows, width)

    def send_back(terms):
        if not fine:
            terms = terms.reshape(window, n_all, piece, width).transpose(1, 0, 2, 3)
        terms = lax.all_to_all(terms, both, 0, 0, tiled=True)
        summed = small_call(
            functools.partial(sum_kernel, window),
            "sum_terms",
            shape_of((n_ctx, n_head, piece, width), BF16),
            n_ctx,
        )(tile_of, terms.reshape(n_ctx, n_head, window, piece, width))
        result = lax.all_to_all(
            summed.reshape(n_all, piece, width), both, 0, 0, tiled=True
        )
        return result.reshape(tile_rows, width)

    held_keys = spread(keys)
    held_values = spread(values)
    past_keys = fetch(held_keys)
    past_values = fetch(held_values)

    q_turned, g_turned, own_weight, own_out, own_stats = chunked_call(
        functools.partial(own_forward_kernel, heads),
        "own_forward",
        row_total,
        [rows_of(width), rows_of(width), whole((tile_rows, width)), whole((tile_rows, width))],
        (
            columns_of(width),
            columns_of(width),
            columns_of(tile_rows),
            columns_of(width),
            columns_of(8),
        ),
        (
            shape_of((width, row_total), BF16),
            shape_of((width, row_total), BF16),
            shape_of((tile_rows, row_total), BF16),
            shape_of((width, row_total), F32),
            shape_of((8, row_total), F32),
        ),
        [pltpu.VMEM((width, tile_rows), BF16), pltpu.VMEM((tile_rows, ROW_BLOCK), F32)],
        2 * work,
    )(*scalars, q_rows, g_rows, keys, values)

    prob, stats, dv_terms = chunked_call(
        functools.partial(past_weights_kernel, window, heads, tile_rows),
        "past_weights",
        row_total,
        [columns_of(width), rows_of(width), columns_of(8), whole(pieces_shape)],
        (columns_of(past_rows), columns_of(8), whole(pieces_shape)),
        (
            shape_of((past_rows, row_total), BF16),
            shape_of((8, row_total), F32),
            shape_of(pieces_shape, BF16),
        ),
        [
            pltpu.VMEM((past_rows, width), BF16),
            pltpu.VMEM((past_rows, ROW_BLOCK), F32),
            pltpu.VMEM((past_rows, width), F32),
        ],
        2 * window * work,
    )(*scalars, q_turned, g_rows, own_stats, past_keys)

    attended, delta, past_dq, dk_terms = chunked_call(
        functools.partial(past_grads_kernel, window, heads, tile_rows),
        "past_grads",
        row_total,
        [
            rows_of(width),
            columns_of(width),
            columns_of(past_rows),
            columns_of(8),
            columns_of(width),
            whole(pieces_shape),
            whole(pieces_shape),
        ],
        (rows_of(width), columns_of(8), columns_of(width), whole(pieces_shape)),
        (
            shape_of((row_total, width), BF16),
            shape_of((8, row_total), F32),
            shape_of((width, row_total), F32),
            shape_of(pieces_shape, BF16),
        ),
        [
            pltpu.VMEM((past_rows, width), BF16),
            pltpu.VMEM((past_rows, width), BF16),
            pltpu.VMEM((width, past_rows), BF16),
            pltpu.VMEM((width, past_rows), BF16),
            pltpu.VMEM((past_rows, width), F32),
        ],
        4 * window * work,
    )(*scalars, q_rows, g_turned, prob, stats, own_out, past_keys, past_values)

    query_grad, own_grads = chunked_call(
        functools.partial(own_grads_kernel, heads),
        "own_grads",
        row_total,
        [
            rows_of(width),
            rows_of(width),
            columns_of(width),
            columns_of(tile_rows),
            columns_of(8),
            columns_of(8),
            columns_of(width),
            whole((tile_rows, width)),
            whole((tile_rows, width)),
        ],
        (rows_of(width), whole((2, tile_rows, width))),
        (
            shape_of((row_total, width), BF16),
            shape_of((2, tile_rows, width), BF16),
        ),
        [
            pltpu.VMEM((width, tile_rows), BF16),
            pltpu.VMEM((tile_rows, width), F32),
            pltpu.VMEM((tile_rows, width), F32),
        ],
        4 * work,
    )(*scalars, q_rows, g_rows, g_turned, own_weight, stats, delta, past_dq, keys, values)

    far_values = send_back(dv_terms)
    far_keys = send_back(dk_terms)
    if n_head == 2:
        peer = lax.ppermute(own_grads, "head", [(0, 1), (1, 0)])
        near = own_grads.astype(F32) + peer.astype(F32)
    else:
        near = lax.psum(own_grads.astype(F32), "head")
    return (
        attended.reshape(tile_rows, heads, width),
        query_grad.reshape(tile_rows, heads, width),
        near[0] + far_keys.astype(F32),
        near[1] + far_values.astype(F32),
    )


def solution(mesh):
    return jax.shard_map(
        on_device,
        mesh=mesh,
        in_specs=(
            P("ctx", "head", None),
            P("ctx", None),
            P("ctx", None),
            P("ctx", "head", None),
            P(),
            P(),
        ),
        out_specs=(P("ctx", "head", None), P("ctx", "head", None), P("ctx", None), P("ctx", None)),
        check_vma=False,
    )
```

profile of v0, /device:TPU:0, one launch (start us, length us, event | category | flops | bytes accessed | tf_op | source)
XLA Modules:
  0.0 151.3 jit_solution(12745420861242868334)
XLA Ops:
  0.6 0.0 copy-start.3
  0.6 1.6 %dynamic-slice_bitcast_fusion.1 = bf16[16,16,128]{2,1,0:T(8,128)(2,1)} fusion(bf16[16,2,16,128]{3,2,1,0:T(8,128)(2,1)} %bitcast.41, s32[]{:T(128)S(6)} %select_n.5), kind=kLoop, calls=%fused_computation.6 | loop fusion | bytes 131076 | tf_op jit(solution)/shard_map/jit(dynamic_index_in_dim)/squeeze | solution.py:474
  2.2 7.4 %all-to-all-start = ((bf16[16,16,128]{2,1,0:T(8,128)(2,1)}), bf16[16,16,128]{2,1,0:T(8,128)(2,1)S(1)}, u32[]{:S(2)}, u32[]{:S(2)}) async-start(bf16[16,16,128]{2,1,0:T(8,128)(2,1)} %dynamic-slice_bitcast_fusion.1), calls=%async_computation | async-start | bytes 131072 | tf_op jit(solution)/shard_map/all_to_all | solution.py:475
  9.6 1.5 dynamic-slice_bitcast_fusion
  11.1 5.4 %all-to-all-done.held_ref = bf16[16,16,128]{2,1,0:T(8,128)(2,1)S(1)} async-done(((bf16[16,16,128]{2,1,0:T(8,128)(2,1)}), bf16[16,16,128]{2,1,0:T(8,128)(2,1)S(1)}, u32[]{:S(2)}, u32[]{:S(2)}) %all-to-all-start) | async-done | bytes 65568 | tf_op jit(solution)/shard_map/all_to_all | solution.py:475
  16.5 3.5 %all-to-all-start.2 = ((bf16[16,16,128]{2,1,0:T(8,128)(2,1)}), bf16[16,16,128]{2,1,0:T(8,128)(2,1)S(1)}, u32[]{:S(2)}, u32[]{:S(2)}) async-start(bf16[16,16,128]{2,1,0:T(8,128)(2,1)} %dynamic-slice_bitcast_fusion), calls=%async_computation.2 | async-start | bytes 131072 | tf_op jit(solution)/shard_map/all_to_all | solution.py:475
  20.0 0.0 copy-done.23
  20.0 1.8 %route.2 = bf16[16,2,2,16,128]{4,3,2,1,0:T(8,128)(2,1)} custom-call(s32[16]{0:T(128)} %tile_of_ref.15, bf16[16,16,128]{2,1,0:T(8,128)(2,1)} %copy-done.23), custom_call_target="tpu_custom_call" | custom-call | tf_op jit(solution)/shard_map/route/pallas_call | solution.py:478
  21.8 5.1 %all-to-all-done.2.held_ref = bf16[16,16,128]{2,1,0:T(8,128)(2,1)S(1)} async-done(((bf16[16,16,128]{2,1,0:T(8,128)(2,1)}), bf16[16,16,128]{2,1,0:T(8,128)(2,1)S(1)}, u32[]{:S(2)}, u32[]{:S(2)}) %all-to-all-start.2) | async-done | bytes 65568 | tf_op jit(solution)/shard_map/all_to_all | solution.py:475
  26.8 2.6 %all-to-all-start.1 = ((bf16[32,2,16,128]{3,2,1,0:T(8,128)(2,1)}), bf16[32,2,16,128]{3,2,1,0:T(8,128)(2,1)S(1)}, u32[]{:S(2)}, u32[]{:S(2)}) async-start(bf16[32,2,16,128]{3,2,1,0:T(8,128)(2,1)} %bitcast.44), calls=%async_computation.1 | async-start | bytes 524288 | tf_op jit(solution)/shard_map/all_to_all | solution.py:484
  29.5 1.8 %route.3 = bf16[16,2,2,16,128]{4,3,2,1,0:T(8,128)(2,1)} custom-call(s32[16]{0:T(128)} %tile_of_ref.15, bf16[16,16,128]{2,1,0:T(8,128)(2,1)} %copy-done.24), custom_call_target="tpu_custom_call" | custom-call | tf_op jit(solution)/shard_map/route/pallas_call | solution.py:478
  31.2 8.9 %all-to-all-done.1.past_keys_ref = bf16[32,2,16,128]{3,2,1,0:T(8,128)(2,1)S(1)} async-done(((bf16[32,2,16,128]{3,2,1,0:T(8,128)(2,1)}), bf16[32,2,16,128]{3,2,1,0:T(8,128)(2,1)S(1)}, u32[]{:S(2)}, u32[]{:S(2)}) %all-to-all-start.1) | async-done | bytes 262176 | tf_op jit(solution)/shard_map/all_to_all | solution.py:484
  40.1 2.6 %all-to-all-start.3 = ((bf16[32,2,16,128]{3,2,1,0:T(8,128)(2,1)}), bf16[32,2,16,128]{3,2,1,0:T(8,128)(2,1)S(1)}, u32[]{:S(2)}, u32[]{:S(2)}) async-start(bf16[32,2,16,128]{3,2,1,0:T(8,128)(2,1)} %bitcast.43), calls=%async_computation.3 | async-start | bytes 524288 | tf_op jit(solution)/shard_map/all_to_all | solution.py:484
  42.7 0.0 copy-start
  42.7 1.2 copy-done
  44.0 1.2 copy-done.2
  45.2 0.9 copy-done.8
  46.1 0.9 copy-done.10
  47.0 0.7 copy-done.19
  47.7 0.7 copy-done.21
  48.3 9.1 %own_forward.1 = (bf16[128,4096]{1,0:T(8,128)(2,1)S(1)}, bf16[128,4096]{1,0:T(8,128)(2,1)S(1)}, bf16[512,4096]{1,0:T(8,128)(2,1)}, f32[128,4096]{1,0:T(8,128)}, f32[8,4096]{1,0:T(8,128)S(1)}) custom-call(s32[1]{0:T(128)} %bitcast.place_ref, s32[16]{0:T(128)S(1)} %copy-done.21, s32[16]{0:T(128)S(1)} %copy-done.19, bf16[4096,128]{1,0:T(8,128)(2,1)S(1)} %bitcast.35, ...), custom_call_target="tpu_custom_call" | custom-call | flops 1073741824 | bytes 4194304 | tf_op jit(solution)/shard_map/own_forward/pallas_call | solution.py:513
  57.4 1.0 copy-done.5
  58.4 7.6 %past_weights.1 = (bf16[1024,4096]{1,0:T(8,128)(2,1)}, f32[8,4096]{1,0:T(8,128)S(1)}, bf16[32,2,16,128]{3,2,1,0:T(8,128)(2,1)S(1)}) custom-call(s32[1]{0:T(128)} %bitcast.place_ref, s32[16]{0:T(128)S(1)} %copy-done.21, s32[16]{0:T(128)S(1)} %copy-done.19, bf16[128,4096]{1,0:T(8,128)(2,1)S(1)} %get-tuple-element.19.q_turned_ref, ...), custom_call_target="tpu_custom_call" | custom-call | flops 2147483648 | bytes 4194304 | tf_op jit(solution)/shard_map/past_weights/pallas_call | solution.py:536
  65.9 0.7 copy-done.14
  66.7 0.0 all-to-all-done.3.past_values_ref
  66.7 0.7 copy-done.15
  67.4 1.2 copy-done.6
  68.6 0.9 copy-done.13
  69.6 0.9 copy-done.16
  70.5 10.2 %past_grads.1 = (bf16[4096,128]{1,0:T(8,128)(2,1)}, f32[8,4096]{1,0:T(8,128)S(1)}, f32[128,4096]{1,0:T(8,128)S(1)}, bf16[32,2,16,128]{3,2,1,0:T(8,128)(2,1)S(1)}) custom-call(s32[1]{0:T(128)} %bitcast.place_ref, s32[16]{0:T(128)S(1)} %copy-done.22, s32[16]{0:T(128)S(1)} %copy-done.20, bf16[4096,128]{1,0:T(8,128)(2,1)S(1)} %bitcast.36, ...), custom_call_target="tpu_custom_call" | custom-call | flops 4294967296 | bytes 4194304 | tf_op jit(solution)/shard_map/past_grads/pallas_call | solution.py:555
  80.7 25.3 %all_to_all.40 = bf16[32,2,16,128]{3,2,1,0:T(8,128)(2,1)} all-to-all(bf16[32,2,16,128]{3,2,1,0:T(8,128)(2,1)S(1)} %get-tuple-element.30), channel_id=1, replica_groups=mesh['ctx'=16,'head'=2] {'ctx','head'}, dimensions={0} | all-to-all | bytes 524288 | tf_op jit(solution)/shard_map/all_to_all | solution.py:496
  105.9 3.3 %all-to-all-start.6 = ((bf16[32,2,16,128]{3,2,1,0:T(8,128)(2,1)}), bf16[32,2,16,128]{3,2,1,0:T(8,128)(2,1)}, u32[]{:S(2)}, u32[]{:S(2)}) async-start(bf16[32,2,16,128]{3,2,1,0:T(8,128)(2,1)} %copy-done.14), calls=%async_computation.6 | async-start | bytes 524288 | tf_op jit(solution)/shard_map/all_to_all | solution.py:496
  109.3 0.0 copy-start.4
  109.3 1.2 copy-done.4
  110.5 1.2 copy-done.7
  111.7 0.9 copy-done.18
  112.6 9.3 %own_grads.1 = (bf16[4096,128]{1,0:T(8,128)(2,1)}, bf16[2,512,128]{2,1,0:T(8,128)(2,1)}) custom-call(s32[1]{0:T(128)} %bitcast.place_ref, s32[16]{0:T(128)S(1)} %copy-done.22, s32[16]{0:T(128)S(1)} %copy-done.20, bf16[4096,128]{1,0:T(8,128)(2,1)S(1)} %bitcast.37, bf16[4096,128]{1,0:T(8,128)(2,1)S(1)} %bitcast.40, bf16[128,4096]{1,0:T(8,128)(2,1)S(1)} %copy-done.7, ...), custom_call_target="tpu_custom_call" | custom-call | flops 2147483648 | bytes 4194304 | tf_op jit(solution)/shard_map/own_grads/pallas_call | solution.py:585
  122.0 1.6 %collective-permute-start = (bf16[2,512,128]{2,1,0:T(8,128)(2,1)}, bf16[2,512,128]{2,1,0:T(8,128)(2,1)S(1)}, u32[]{:S(2)}, u32[]{:S(2)}) collective-permute-start(bf16[2,512,128]{2,1,0:T(8,128)(2,1)} %get-tuple-element.29), channel_id=1, source_target_pairs={{0,1},{1,0},{2,3},{3,2},{4,5},{5,4},{6,7},{7,6},{8,9},{9,8},{10,11... | collective-permute-start | bytes 786440 | tf_op jit(solution)/shard_map/ppermute | solution.py:616
  123.5 1.9 %sum_terms.2 = bf16[16,2,16,128]{3,2,1,0:T(8,128)(2,1)} custom-call(s32[16]{0:T(128)} %tile_of_ref.15, bf16[16,2,2,16,128]{4,3,2,1,0:T(8,128)(2,1)} %bitcast.45), custom_call_target="tpu_custom_call" | custom-call | tf_op jit(solution)/shard_map/sum_terms/pallas_call | solution.py:497
  125.4 0.0 all-to-all-done.6
  125.4 5.2 %all-to-all-start.5 = ((bf16[32,16,128]{2,1,0:T(8,128)(2,1)}), bf16[32,16,128]{2,1,0:T(8,128)(2,1)S(1)}, u32[]{:S(2)}, u32[]{:S(2)}) async-start(bf16[32,16,128]{2,1,0:T(8,128)(2,1)} %bitcast.47), calls=%async_computation.5 | async-start | bytes 262144 | tf_op jit(solution)/shard_map/all_to_all | solution.py:503
  130.7 1.9 %sum_terms.3 = bf16[16,2,16,128]{3,2,1,0:T(8,128)(2,1)} custom-call(s32[16]{0:T(128)} %tile_of_ref.15, bf16[16,2,2,16,128]{4,3,2,1,0:T(8,128)(2,1)} %bitcast.16.terms_ref), custom_call_target="tpu_custom_call" | custom-call | tf_op jit(solution)/shard_map/sum_terms/pallas_call | solution.py:497
  132.6 6.7 %all-to-all-done.5 = bf16[32,16,128]{2,1,0:T(8,128)(2,1)S(1)} async-done(((bf16[32,16,128]{2,1,0:T(8,128)(2,1)}), bf16[32,16,128]{2,1,0:T(8,128)(2,1)S(1)}, u32[]{:S(2)}, u32[]{:S(2)}) %all-to-all-start.5) | async-done | bytes 131104 | tf_op jit(solution)/shard_map/all_to_all | solution.py:503
  139.3 2.6 %all-to-all-start.7 = ((bf16[32,16,128]{2,1,0:T(8,128)(2,1)}), bf16[32,16,128]{2,1,0:T(8,128)(2,1)S(1)}, u32[]{:S(2)}, u32[]{:S(2)}) async-start(bf16[32,16,128]{2,1,0:T(8,128)(2,1)} %bitcast.46), calls=%async_computation.7 | async-start | bytes 262144 | tf_op jit(solution)/shard_map/all_to_all | solution.py:503
  141.9 0.0 collective-permute-done
  141.9 1.0 convert_add_fusion
  142.9 7.6 %all-to-all-done.7 = bf16[32,16,128]{2,1,0:T(8,128)(2,1)S(1)} async-done(((bf16[32,16,128]{2,1,0:T(8,128)(2,1)}), bf16[32,16,128]{2,1,0:T(8,128)(2,1)S(1)}, u32[]{:S(2)}, u32[]{:S(2)}) %all-to-all-start.7) | async-done | bytes 131104 | tf_op jit(solution)/shard_map/all_to_all | solution.py:503
  150.5 0.8 fusion
  (31 shorter events, 0.1 us)
Async XLA Ops:
  0.6 57.7 %copy-start.3 = (bf16[512,8,128]{2,1,0:T(8,128)(2,1)S(1)}, bf16[512,8,128]{2,1,0:T(8,128)(2,1)}, u32[]{:S(2)}) copy-start(bf16[512,8,128]{2,1,0:T(8,128)(2,1)} %param.9) | copy-start | bytes 3145732
  2.2 14.3 %all-to-all-start = ((bf16[16,16,128]{2,1,0:T(8,128)(2,1)}), bf16[16,16,128]{2,1,0:T(8,128)(2,1)S(1)}, u32[]{:S(2)}, u32[]{:S(2)}) async-start(bf16[16,16,128]{2,1,0:T(8,128)(2,1)} %dynamic-slice_bitcast_fusion.1), calls=%async_computation | async-start | bytes 131072 | tf_op jit(solution)/shard_map/all_to_all | solution.py:475
  16.5 3.5 %copy-start.23 = (bf16[16,16,128]{2,1,0:T(8,128)(2,1)}, bf16[16,16,128]{2,1,0:T(8,128)(2,1)S(1)}, u32[]{:S(2)}) copy-start(bf16[16,16,128]{2,1,0:T(8,128)(2,1)S(1)} %all-to-all-done.held_ref) | copy-start | bytes 196612
  16.5 10.4 %all-to-all-start.2 = ((bf16[16,16,128]{2,1,0:T(8,128)(2,1)}), bf16[16,16,128]{2,1,0:T(8,128)(2,1)S(1)}, u32[]{:S(2)}, u32[]{:S(2)}) async-start(bf16[16,16,128]{2,1,0:T(8,128)(2,1)} %dynamic-slice_bitcast_fusion), calls=%async_computation.2 | async-start | bytes 131072 | tf_op jit(solution)/shard_map/all_to_all | solution.py:475
  26.8 2.6 %copy-start.24 = (bf16[16,16,128]{2,1,0:T(8,128)(2,1)}, bf16[16,16,128]{2,1,0:T(8,128)(2,1)S(1)}, u32[]{:S(2)}) copy-start(bf16[16,16,128]{2,1,0:T(8,128)(2,1)S(1)} %all-to-all-done.2.held_ref) | copy-start | bytes 196612
  26.8 13.3 %all-to-all-start.1 = ((bf16[32,2,16,128]{3,2,1,0:T(8,128)(2,1)}), bf16[32,2,16,128]{3,2,1,0:T(8,128)(2,1)S(1)}, u32[]{:S(2)}, u32[]{:S(2)}) async-start(bf16[32,2,16,128]{3,2,1,0:T(8,128)(2,1)} %bitcast.44), calls=%async_computation.1 | async-start | bytes 524288 | tf_op jit(solution)/shard_map/all_to_all | solution.py:484
  40.1 25.8 %copy-start.12 = (bf16[32,2,16,128]{3,2,1,0:T(8,128)(2,1)}, bf16[32,2,16,128]{3,2,1,0:T(8,128)(2,1)S(1)}, u32[]{:S(2)}) copy-start(bf16[32,2,16,128]{3,2,1,0:T(8,128)(2,1)S(1)} %all-to-all-done.1.past_keys_ref) | copy-start | bytes 786436
  40.1 26.5 %all-to-all-start.3 = ((bf16[32,2,16,128]{3,2,1,0:T(8,128)(2,1)}), bf16[32,2,16,128]{3,2,1,0:T(8,128)(2,1)S(1)}, u32[]{:S(2)}, u32[]{:S(2)}) async-start(bf16[32,2,16,128]{3,2,1,0:T(8,128)(2,1)} %bitcast.43), calls=%async_computation.3 | async-start | bytes 524288 | tf_op jit(solution)/shard_map/all_to_all | solution.py:484
  42.7 1.2 copy-start
  44.0 1.2 copy-start.2
  45.2 0.9 copy-start.8
  46.1 0.9 copy-start.10
  47.0 0.7 copy-start.19
  47.7 0.7 copy-start.21
  57.4 1.0 copy-start.5
  58.4 9.0 %copy-start.1 = (bf16[512,8,128]{2,1,0:T(8,128)(2,1)S(1)}, bf16[512,8,128]{2,1,0:T(8,128)(2,1)}, u32[]{:S(2)}) copy-start(bf16[512,8,128]{2,1,0:T(8,128)(2,1)} %param.6) | copy-start | bytes 3145732
  58.4 9.0 %copy-start.20 = (s32[16]{0:T(128)S(1)}, s32[16]{0:T(128)}, u32[]{:S(2)}) copy-start(s32[16]{0:T(128)} %tile_of_ref.15) | copy-start | bytes 196
  58.4 9.0 %copy-start.22 = (s32[16]{0:T(128)S(1)}, s32[16]{0:T(128)}, u32[]{:S(2)}) copy-start(s32[16]{0:T(128)} %lengths_ref.7) | copy-start | bytes 196
  65.9 0.7 copy-start.14
  66.7 0.7 copy-start.15
  67.4 1.2 copy-start.6
  68.6 0.9 copy-start.13
  69.5 0.9 copy-start.16
  70.5 38.8 %copy-start.9 = (bf16[512,128]{1,0:T(8,128)(2,1)S(1)}, bf16[512,128]{1,0:T(8,128)(2,1)}, u32[]{:S(2)}) copy-start(bf16[512,128]{1,0:T(8,128)(2,1)} %k_ref.3) | copy-start | bytes 393220
  70.5 38.8 %copy-start.11 = (bf16[512,128]{1,0:T(8,128)(2,1)S(1)}, bf16[512,128]{1,0:T(8,128)(2,1)}, u32[]{:S(2)}) copy-start(bf16[512,128]{1,0:T(8,128)(2,1)} %v_ref.3) | copy-start | bytes 393220
  80.7 25.3 %copy-start.17 = (f32[8,4096]{1,0:T(8,128)}, f32[8,4096]{1,0:T(8,128)S(1)}, u32[]{:S(2)}) copy-start(f32[8,4096]{1,0:T(8,128)S(1)} %get-tuple-element.26.delta_ref) | copy-start | bytes 393220
  105.9 19.5 %all-to-all-start.6 = ((bf16[32,2,16,128]{3,2,1,0:T(8,128)(2,1)}), bf16[32,2,16,128]{3,2,1,0:T(8,128)(2,1)}, u32[]{:S(2)}, u32[]{:S(2)}) async-start(bf16[32,2,16,128]{3,2,1,0:T(8,128)(2,1)} %copy-done.14), calls=%async_computation.6 | async-start | bytes 524288 | tf_op jit(solution)/shard_map/all_to_all | solution.py:496
  109.3 1.2 copy-start.4
  110.5 1.2 copy-start.7
  111.7 0.9 copy-start.18
  122.0 19.9 %collective-permute-start = (bf16[2,512,128]{2,1,0:T(8,128)(2,1)}, bf16[2,512,128]{2,1,0:T(8,128)(2,1)S(1)}, u32[]{:S(2)}, u32[]{:S(2)}) collective-permute-start(bf16[2,512,128]{2,1,0:T(8,128)(2,1)} %get-tuple-element.29), channel_id=1, source_target_pairs={{0,1},{1,0},{2,3},{3,2},{4,5},{5,4},{6,7},{7,6},{8,9},{9,8},{10,11... | collective-permute-start | bytes 786440 | tf_op jit(solution)/shard_map/ppermute | solution.py:616
  125.4 13.8 %all-to-all-start.5 = ((bf16[32,16,128]{2,1,0:T(8,128)(2,1)}), bf16[32,16,128]{2,1,0:T(8,128)(2,1)S(1)}, u32[]{:S(2)}, u32[]{:S(2)}) async-start(bf16[32,16,128]{2,1,0:T(8,128)(2,1)} %bitcast.47), calls=%async_computation.5 | async-start | bytes 262144 | tf_op jit(solution)/shard_map/all_to_all | solution.py:503
  139.3 11.2 %all-to-all-start.7 = ((bf16[32,16,128]{2,1,0:T(8,128)(2,1)}), bf16[32,16,128]{2,1,0:T(8,128)(2,1)S(1)}, u32[]{:S(2)}, u32[]{:S(2)}) async-start(bf16[32,16,128]{2,1,0:T(8,128)(2,1)} %bitcast.46), calls=%async_computation.7 | async-start | bytes 262144 | tf_op jit(solution)/shard_map/all_to_all | solution.py:503
where the time goes:
time: 154 us; the launch traced here: 151 us
  Pallas kernels  43.5 us (28%)
  waiting for transfers between devices  33.7 us (22%)
  starting transfers between devices  28.7 us (19%)
  blocking collectives  25.3 us (16%)
  local copies, waits for them, and re-layouts  17.5 us (11%)
  other arithmetic  1.86 us (1%)
    all_to_all x1, blocking collectives, send_back(): terms = lax.all_to_all(terms, both, 0, 0, tiled=True)  25.3 us
    unnamed x50, local copies, waits for them, and re-layouts  14.5 us
    all_to_all x2, waiting for transfers between devices, send_back(): lax.all_to_all(summed.reshape(n_all, piece, width), both, 0, 0, tiled=True)  14.3 us
    all_to_all x2, starting transfers between devices, spread(): return lax.all_to_all(mine, 'ctx', 0, 0, tiled=True)  10.9 us
    all_to_all x2, waiting for transfers between devices, spread(): return lax.all_to_all(mine, 'ctx', 0, 0, tiled=True)  10.5 us
    pallas_call x1, Pallas kernels, on_device(): chunked_call(functools.partial(past_grads_kernel, window, heads, tile_row...  10.2 us
    pallas_call x1, Pallas kernels, on_device(): chunked_call(functools.partial(own_grads_kernel, heads), 'own_grads', row...  9.34 us
    pallas_call x1, Pallas kernels, on_device(): chunked_call(functools.partial(own_forward_kernel, heads), 'own_forward',...  9.09 us
  transfers between devices with their start and end apart: 8, of which 5 were waited for; matrix products, arithmetic and copies ran while one was open for 2% of the time, Pallas kernels for 22%

commit v1 on v0

v1 whole, which is shorter than its diff:
```python
import functools

import jax
import jax.numpy as jnp
from jax import lax
from jax.experimental import pallas as pl
from jax.experimental.pallas import tpu as pltpu
from jax.sharding import PartitionSpec as P

LOG2E = 1.4426950408889634
NEG_FILL = -1e30
KEY_BLOCK = 128
ROW_BLOCK = 512
VMEM_LIMIT = 60 * 1024 * 1024
SMEM = pl.BlockSpec(memory_space=pltpu.SMEM)
F32 = jnp.float32
BF16 = jnp.bfloat16


def matmul(left, right):
    return lax.dot_general(left, right, (((1,), (0,)), ((), ())), preferred_element_type=F32)


def fold_rows(block, combine):
    folded = block[0:8]
    for begin in range(8, block.shape[0], 8):
        folded = combine(folded, block[begin : begin + 8])
    return folded


def document_starts(ends, positions):
    start = jnp.zeros_like(positions)
    for end in ends:
        start = jnp.where(end <= positions, end, start)
    return start


def document_ends(lengths_ref):
    ends = []
    total = jnp.int32(0)
    for doc in range(lengths_ref.shape[0]):
        total = total + lengths_ref[doc]
        ends.append(total)
    return ends


def lane_positions(heads, first_pos):
    lane = lax.broadcasted_iota(jnp.int32, (1, ROW_BLOCK), 1)
    return first_pos + lax.div(lane, heads)


def key_positions(begin):
    return begin + lax.broadcasted_iota(jnp.int32, (KEY_BLOCK, ROW_BLOCK), 0)


def fold_all(blocks, combine):
    folded = fold_rows(blocks[0], combine)
    for block in blocks[1:]:
        folded = combine(folded, fold_rows(block, combine))
    return folded


def own_extents(heads, tile_rows):
    chunk_pos = ROW_BLOCK // heads
    ends = [-(-(begin + chunk_pos) // KEY_BLOCK) for begin in range(0, tile_rows, chunk_pos)]
    return sorted(set(ends))


def by_extent(heads, tile_rows, branch):
    chunk_pos = ROW_BLOCK // heads
    extents = own_extents(heads, tile_rows)
    end = lax.div((pl.program_id(0) + 1) * chunk_pos - 1, KEY_BLOCK) + 1
    for extent in extents:
        pl.when(end == extent)(functools.partial(branch, extent))


def own_forward_kernel(
    heads,
    place_ref,
    lengths_ref,
    tile_of_ref,
    q_ref,
    g_ref,
    k_ref,
    v_ref,
    q_turned_ref,
    g_turned_ref,
    weight_ref,
    out_ref,
    stats_ref,
    v_turned,
):
    tile_rows, width = k_ref.shape
    exponent_scale = float(width) ** (-0.5) * LOG2E

    @pl.when(pl.program_id(0) == 0)
    def turn_values():
        v_turned[...] = v_ref[...].T

    tile_begin = tile_of_ref[place_ref[0]] * tile_rows
    first_pos = tile_begin + pl.program_id(0) * (ROW_BLOCK // heads)
    q_turned = q_ref[...].T
    q_turned_ref[...] = q_turned
    g_turned_ref[...] = g_ref[...].T
    q_pos = lane_positions(heads, first_pos)
    low = document_starts(document_ends(lengths_ref), q_pos) - tile_begin
    high = q_pos - tile_begin

    def branch(extent):
        scores = []
        for block in range(extent):
            begin = block * KEY_BLOCK
            score = matmul(k_ref[begin : begin + KEY_BLOCK, :], q_turned)
            key_pos = key_positions(begin)
            live = key_pos >= low
            if block == extent - 1:
                live = live & (key_pos <= high)
            scores.append(jnp.where(live, score, NEG_FILL))
        top = jnp.max(fold_all(scores, jnp.maximum), axis=0, keepdims=True) * exponent_scale
        weights = [jnp.exp2(score * exponent_scale - top) for score in scores]
        out_turned = jnp.zeros((width, ROW_BLOCK), F32)
        for block in range(extent):
            begin = block * KEY_BLOCK
            weight_low = weights[block].astype(BF16)
            weight_ref[begin : begin + KEY_BLOCK, :] = weight_low
            out_turned += matmul(v_turned[:, begin : begin + KEY_BLOCK], weight_low)
        out_ref[...] = out_turned
        stats_ref[0:1, :] = top
        stats_ref[1:2, :] = jnp.sum(fold_all(weights, jnp.add), axis=0, keepdims=True)

    by_extent(heads, tile_rows, branch)


def past_kernel(
    window,
    heads,
    tile_rows,
    place_ref,
    lengths_ref,
    tile_of_ref,
    q_ref,
    g_ref,
    q_turned_ref,
    g_turned_ref,
    own_stats_ref,
    own_out_ref,
    past_ref,
    att_ref,
    dq_ref,
    grads_ref,
    stats_ref,
    k_win,
    v_win,
    k_turned,
    v_turned,
    dk_acc,
    dv_acc,
):
    past_rows, width = k_win.shape
    n_all, _, _, piece, _ = past_ref.shape
    scale = float(width) ** (-0.5)
    exponent_scale = scale * LOG2E
    step = pl.program_id(0)

    @pl.when(step == 0)
    def begin():
        for slot in range(window):
            for owner in range(n_all):
                row = slot * tile_rows + owner * piece
                k_win[row : row + piece, :] = past_ref[owner, slot, 0]
                v_win[row : row + piece, :] = past_ref[owner, slot, 1]
        k_turned[...] = k_win[...].T
        v_turned[...] = v_win[...].T
        dk_acc[...] = jnp.zeros_like(dk_acc)
        dv_acc[...] = jnp.zeros_like(dv_acc)

    base = (tile_of_ref[place_ref[0]] - window) * tile_rows
    first_pos = base + past_rows + step * (ROW_BLOCK // heads)
    ends = document_ends(lengths_ref)
    first_start = jnp.maximum(document_starts(ends, first_pos) - base, 0)
    unit = window * KEY_BLOCK
    branches = past_rows // unit
    live_units = branches - lax.div(jnp.minimum(first_start, past_rows), unit)
    low = document_starts(ends, lane_positions(heads, first_pos)) - base
    own_top = own_stats_ref[0:1, :]
    own_sum = own_stats_ref[1:2, :]

    def finish_chunk(out_turned, dq_turned, rescale, delta):
        att_ref[...] = out_turned.T.astype(BF16)
        dq_ref[...] = dq_turned
        stats_ref[0:1, :] = rescale
        stats_ref[1:2, :] = delta

    def branch(units):
        q_turned = q_turned_ref[...]
        g_turned = g_turned_ref[...]
        begins = range(past_rows - units * unit, past_rows, KEY_BLOCK)
        scores = []
        for begin in begins:
            score = matmul(k_win[begin : begin + KEY_BLOCK, :], q_turned)
            scores.append(jnp.where(key_positions(begin) >= low, score, NEG_FILL))
        top = jnp.max(fold_all(scores, jnp.maximum), axis=0, keepdims=True) * exponent_scale
        top = jnp.maximum(top, own_top)
        weights = [jnp.exp2(score * exponent_scale - top) for score in scores]
        dprobs = [matmul(v_win[begin : begin + KEY_BLOCK, :], g_turned) for begin in begins]
        rescale = jnp.exp2(own_top - top)
        total = own_sum * rescale + jnp.sum(
            fold_all(weights, jnp.add), axis=0, keepdims=True
        )
        inverse = 1.0 / total
        rescale = rescale * inverse
        out_turned = own_out_ref[...] * rescale
        probs = [weight * inverse for weight in weights]
        for begin, prob in zip(begins, probs):
            prob_low = prob.astype(BF16)
            out_turned += matmul(v_turned[:, begin : begin + KEY_BLOCK], prob_low)
            dv_acc[begin : begin + KEY_BLOCK, :] += matmul(prob_low, g_ref[...])
        delta = jnp.sum(out_turned * g_turned.astype(F32), axis=0, keepdims=True)
        dq_turned = jnp.zeros((width, ROW_BLOCK), F32)
        for begin, prob, dprob in zip(begins, probs, dprobs):
            dscore = (prob * (dprob - delta)).astype(BF16)
            dk_acc[begin : begin + KEY_BLOCK, :] += matmul(dscore, q_ref[...])
            dq_turned += matmul(k_turned[:, begin : begin + KEY_BLOCK], dscore)
        finish_chunk(out_turned, dq_turned, rescale, delta)

    @pl.when(live_units == 0)
    def nothing_past():
        rescale = 1.0 / own_sum
        out_turned = own_out_ref[...] * rescale
        delta = jnp.sum(out_turned * g_turned_ref[...].astype(F32), axis=0, keepdims=True)
        finish_chunk(out_turned, jnp.zeros((width, ROW_BLOCK), F32), rescale, delta)

    for units in range(1, branches + 1):
        pl.when(live_units == units)(functools.partial(branch, units))

    @pl.when(step == pl.num_programs(0) - 1)
    def finish():
        for slot in range(window):
            for owner in range(n_all):
                row = slot * tile_rows + owner * piece
                grads_ref[owner, slot, 0] = (dk_acc[row : row + piece, :] * scale).astype(BF16)
                grads_ref[owner, slot, 1] = dv_acc[row : row + piece, :].astype(BF16)


def own_grads_kernel(
    heads,
    q_ref,
    g_ref,
    g_turned_ref,
    weight_ref,
    stats_ref,
    past_dq_ref,
    k_ref,
    v_ref,
    dq_ref,
    dkv_ref,
    k_turned,
    dk_acc,
    dv_acc,
):
    tile_rows, width = k_ref.shape
    scale = float(width) ** (-0.5)

    @pl.when(pl.program_id(0) == 0)
    def begin():
        k_turned[...] = k_ref[...].T
        dk_acc[...] = jnp.zeros_like(dk_acc)
        dv_acc[...] = jnp.zeros_like(dv_acc)

    rescale = stats_ref[0:1, :]
    delta = stats_ref[1:2, :]

    def branch(extent):
        q_rows = q_ref[...]
        g_rows = g_ref[...]
        g_turned = g_turned_ref[...]
        dq_turned = past_dq_ref[...]
        for block in range(extent):
            begin = block * KEY_BLOCK
            keys = slice(begin, begin + KEY_BLOCK)
            prob = weight_ref[keys, :].astype(F32) * rescale
            dprob = matmul(v_ref[keys, :], g_turned)
            dscore = (prob * (dprob - delta)).astype(BF16)
            dv_acc[keys, :] += matmul(prob.astype(BF16), g_rows)
            dk_acc[keys, :] += matmul(dscore, q_rows)
            dq_turned += matmul(k_turned[:, keys], dscore)
        dq_ref[...] = (dq_turned * scale).T.astype(BF16)

    by_extent(heads, tile_rows, branch)

    @pl.when(pl.program_id(0) == pl.num_programs(0) - 1)
    def finish():
        dkv_ref[0] = (dk_acc[...] * scale).astype(BF16)
        dkv_ref[1] = dv_acc[...].astype(BF16)


def route_kernel(window, tile_of_ref, held_ref, out_ref, holder):
    n_ctx, n_head = out_ref.shape[:2]
    for ctx in range(n_ctx):
        holder[tile_of_ref[ctx]] = ctx

    def one(ctx, carry):
        for slot in range(window):
            tile = tile_of_ref[ctx] - (window - slot)
            source = holder[jnp.maximum(tile, 0)]
            rows = held_ref[source]
            for head in range(n_head):
                out_ref[ctx, head, slot] = rows
        return carry

    lax.fori_loop(0, n_ctx, one, 0)


def sum_kernel(window, tile_of_ref, terms_ref, out_ref, holder):
    n_ctx, n_head = out_ref.shape[:2]
    for ctx in range(n_ctx):
        holder[tile_of_ref[ctx]] = ctx

    def one(ctx, carry):
        total = jnp.zeros(out_ref.shape[2:], F32)
        for slot in range(window):
            tile = tile_of_ref[ctx] + (window - slot)
            source = holder[jnp.minimum(tile, n_ctx - 1)]
            part = terms_ref[source, 0, slot].astype(F32)
            for head in range(1, n_head):
                part = part + terms_ref[source, head, slot].astype(F32)
            total = total + jnp.where(tile < n_ctx, part, 0.0)
        for head in range(n_head):
            out_ref[ctx, head] = total.astype(BF16)
        return carry

    lax.fori_loop(0, n_ctx, one, 0)


def whole(shape):
    return pl.BlockSpec(shape, lambda chunk: (0,) * len(shape))


def rows_of(width):
    return pl.BlockSpec((ROW_BLOCK, width), lambda chunk: (chunk, 0))


def columns_of(height):
    return pl.BlockSpec((height, ROW_BLOCK), lambda chunk: (0, chunk))


def shape_of(shape, dtype):
    return jax.ShapeDtypeStruct(shape, dtype)


def chunked_call(body, name, scalars, row_total, in_specs, out_specs, out_shape, scratch, flops):
    return pl.pallas_call(
        body,
        grid=(row_total // ROW_BLOCK,),
        in_specs=[SMEM] * scalars + in_specs,
        out_specs=out_specs,
        out_shape=out_shape,
        scratch_shapes=scratch,
        compiler_params=pltpu.CompilerParams(vmem_limit_bytes=VMEM_LIMIT),
        cost_estimate=pl.CostEstimate(
            flops=flops, bytes_accessed=1 << 22, transcendentals=0
        ),
        name=name,
    )


def small_call(body, name, out_shape, n_ctx):
    vmem = pl.BlockSpec(memory_space=pltpu.VMEM)
    return pl.pallas_call(
        body,
        in_specs=[SMEM, vmem],
        out_specs=vmem,
        out_shape=out_shape,
        scratch_shapes=[pltpu.SMEM((n_ctx,), jnp.int32)],
        compiler_params=pltpu.CompilerParams(vmem_limit_bytes=VMEM_LIMIT),
        name=name,
    )


def on_device(queries, keys, values, grad_out, lengths, tile_of):
    tile_rows, heads, width = queries.shape
    n_ctx = lax.axis_size("ctx")
    n_head = lax.axis_size("head")
    n_all = n_ctx * n_head
    piece = tile_rows // n_all
    both = ("ctx", "head")
    most_doc = n_ctx * tile_rows // 8
    window = -(-(most_doc - 1) // tile_rows)
    past_rows = window * tile_rows
    row_total = tile_rows * heads
    place = lax.axis_index("ctx").astype(jnp.int32).reshape(1)
    y = lax.axis_index("head")
    scalars = (place, lengths, tile_of)
    q_rows = queries.reshape(row_total, width)
    g_rows = grad_out.reshape(row_total, width)
    work = 2 * row_total * tile_rows * width
    fine = piece % 16 == 0

    pieces = jnp.stack(
        [tile.reshape(n_ctx, n_head, piece, width) for tile in (keys, values)], axis=2
    )
    mine = lax.dynamic_index_in_dim(pieces, y, 1, keepdims=False)
    held = lax.all_to_all(mine, "ctx", 0, 0, tiled=True)
    packed = small_call(
        functools.partial(route_kernel, window),
        "route",
        shape_of((n_ctx, n_head, window, 2, piece, width), BF16),
        n_ctx,
    )(tile_of, held)
    past = lax.all_to_all(
        packed.reshape(n_all, window, 2, piece, width), both, 0, 0, tiled=True
    )
    pieces_shape = (n_all, window, 2, piece, width)
    if not fine:
        pieces_shape = (1, window, 2, tile_rows, width)
        past = past.transpose(1, 2, 0, 3, 4).reshape(pieces_shape)

    q_turned, g_turned, own_weight, own_out, own_stats = chunked_call(
        functools.partial(own_forward_kernel, heads),
        "own_forward",
        3,
        row_total,
        [rows_of(width), rows_of(width), whole((tile_rows, width)), whole((tile_rows, width))],
        (
            columns_of(width),
            columns_of(width),
            columns_of(tile_rows),
            columns_of(width),
            columns_of(8),
        ),
        (
            shape_of((width, row_total), BF16),
            shape_of((width, row_total), BF16),
            shape_of((tile_rows, row_total), BF16),
            shape_of((width, row_total), F32),
            shape_of((8, row_total), F32),
        ),
        [pltpu.VMEM((width, tile_rows), BF16)],
        2 * work,
    )(*scalars, q_rows, g_rows, keys, values)

    attended, past_dq, terms, stats = chunked_call(
        functools.partial(past_kernel, window, heads, tile_rows),
        "past",
        3,
        row_total,
        [
            rows_of(width),
            rows_of(width),
            columns_of(width),
            columns_of(width),
            columns_of(8),
            columns_of(width),
            whole(pieces_shape),
        ],
        (rows_of(width), columns_of(width), whole(pieces_shape), columns_of(8)),
        (
            shape_of((row_total, width), BF16),
            shape_of((width, row_total), F32),
            shape_of(pieces_shape, BF16),
            shape_of((8, row_total), F32),
        ),
        [
            pltpu.VMEM((past_rows, width), BF16),
            pltpu.VMEM((past_rows, width), BF16),
            pltpu.VMEM((width, past_rows), BF16),
            pltpu.VMEM((width, past_rows), BF16),
            pltpu.VMEM((past_rows, width), F32),
            pltpu.VMEM((past_rows, width), F32),
        ],
        6 * window * work,
    )(*scalars, q_rows, g_rows, q_turned, g_turned, own_stats, own_out, past)

    query_grad, own_grads = chunked_call(
        functools.partial(own_grads_kernel, heads),
        "own_grads",
        0,
        row_total,
        [
            rows_of(width),
            rows_of(width),
            columns_of(width),
            columns_of(tile_rows),
            columns_of(8),
            columns_of(width),
            whole((tile_rows, width)),
            whole((tile_rows, width)),
        ],
        (rows_of(width), whole((2, tile_rows, width))),
        (
            shape_of((row_total, width), BF16),
            shape_of((2, tile_rows, width), BF16),
        ),
        [
            pltpu.VMEM((width, tile_rows), BF16),
            pltpu.VMEM((tile_rows, width), F32),
            pltpu.VMEM((tile_rows, width), F32),
        ],
        4 * work,
    )(q_rows, g_rows, g_turned, own_weight, stats, past_dq, keys, values)

    if not fine:
        terms = terms.reshape(window, 2, n_all, piece, width).transpose(2, 0, 1, 3, 4)
    terms = lax.all_to_all(terms, both, 0, 0, tiled=True)
    summed = small_call(
        functools.partial(sum_kernel, window),
        "sum_terms",
        shape_of((n_ctx, n_head, 2, piece, width), BF16),
        n_ctx,
    )(tile_of, terms.reshape(n_ctx, n_head, window, 2, piece, width))
    far = lax.all_to_all(summed.reshape(n_all, 2, piece, width), both, 0, 0, tiled=True)
    if n_head == 2:
        peer = lax.ppermute(own_grads, "head", [(0, 1), (1, 0)])
        near = own_grads.astype(F32) + peer.astype(F32)
    else:
        near = lax.psum(own_grads.astype(F32), "head")
    far_keys, far_values = (
        far[:, part].reshape(tile_rows, width).astype(F32) for part in range(2)
    )
    return (
        attended.reshape(tile_rows, heads, width),
        query_grad.reshape(tile_rows, heads, width),
        near[0] + far_keys,
        near[1] + far_values,
    )


def solution(mesh):
    return jax.shard_map(
        on_device,
        mesh=mesh,
        in_specs=(
            P("ctx", "head", None),
            P("ctx", None),
            P("ctx", None),
            P("ctx", "head", None),
            P(),
            P(),
        ),
        out_specs=(P("ctx", "head", None), P("ctx", "head", None), P("ctx", None), P("ctx", None)),
        check_vma=False,
    )
```

time: 154 us -> 91.9 us (0.60); the launches traced: 151 us -> 93.4 us
  waiting for transfers between devices: 33.7 us -> 17 us
  local copies, waits for them, and re-layouts: 17.5 us -> 1.62 us
  blocking collectives: 25.3 us -> 15.2 us
  starting transfers between devices: 28.7 us -> 20.5 us
  Pallas kernels: 43.5 us -> 35.7 us
    all_to_all x7 -> x3, waiting for transfers between devices: 33.7 us -> 17 us  [the longest x1 9.67 us: on_device(): lax.all_to_all(summed.reshape(n_all, 2, piece, width), both, 0, 0, tiled=...]
    unnamed x50 -> x4, local copies, waits for them, and re-layouts: 14.5 us -> 1.6 us
    all_to_all x1, blocking collectives: 25.3 us -> 15.2 us  [on_device(): held = lax.all_to_all(mine, 'ctx', 0, 0, tiled=True)]
    pallas_call x7 -> x4, Pallas kernels: 34.4 us -> 25.5 us  [the longest x1 10.8 us: on_device(): chunked_call(functools.partial(past_kernel, window, heads, tile_rows), 'p...]
    all_to_all x7 -> x3, starting transfers between devices: 27.1 us -> 18.6 us  [the longest x1 12.4 us: on_device(): terms = lax.all_to_all(terms, both, 0, 0, tiled=True)]
    squeeze x2 -> x0, local copies, waits for them, and re-layouts: 3.05 us -> none  [spread(): mine = lax.dynamic_index_in_dim(pieces, y, 1, keepdims=False)]
  transfers between devices with their start and end apart: 8 -> 4, of which waited for: 5 -> 3; matrix products, arithmetic and copies ran while one was open for 2% -> 1% of each run, Pallas kernels for 22% -> 24%
where the time goes in v1:
time: 91.9 us; the launch traced here: 93.4 us
  Pallas kernels  35.7 us (39%)
  starting transfers between devices  20.5 us (22%)
  waiting for transfers between devices  17 us (18%)
  blocking collectives  15.2 us (17%)
  other arithmetic  2.75 us (3%)
  local copies, waits for them, and re-layouts  1.62 us (2%)
    all_to_all x1, blocking collectives, on_device(): held = lax.all_to_all(mine, 'ctx', 0, 0, tiled=True)  15.2 us
    all_to_all x1, starting transfers between devices, on_device(): terms = lax.all_to_all(terms, both, 0, 0, tiled=True)  12.4 us
    pallas_call x1, Pallas kernels, on_device(): chunked_call(functools.partial(past_kernel, window, heads, tile_rows), 'p...  10.8 us
    pallas_call x1, Pallas kernels, on_device(): chunked_call(functools.partial(own_grads_kernel, heads), 'own_grads', 0,...  10.7 us
    pallas_call x1, Pallas kernels, on_device(): chunked_call(functools.partial(own_forward_kernel, heads), 'own_forward',...  10.1 us
    all_to_all x1, waiting for transfers between devices, on_device(): lax.all_to_all(summed.reshape(n_all, 2, piece, width), both, 0, 0, tiled=...  9.67 us
    all_to_all x1, waiting for transfers between devices, on_device(): lax.all_to_all(packed.reshape(n_all, window, 2, piece, width), both, 0, 0...  4.84 us
    all_to_all x1, starting transfers between devices, on_device(): lax.all_to_all(summed.reshape(n_all, 2, piece, width), both, 0, 0, tiled=...  3.62 us
  transfers between devices with their start and end apart: 4, of which 3 were waited for; matrix products, arithmetic and copies ran while one was open for 1% of the time, Pallas kernels for 24%

profile of v1, /device:TPU:0, one launch (start us, length us, event | category | flops | bytes accessed | tf_op | source)
XLA Modules:
  0.0 93.4 jit_solution(12019236364009829572)
XLA Ops:
  0.6 0.9 copy_bitcast_fusion
  1.5 15.2 %all_to_all.20.held_ref = bf16[16,2,16,128]{3,2,1,0:T(8,128)(2,1)} all-to-all(bf16[16,2,16,128]{3,2,1,0:T(8,128)(2,1)S(1)} %copy_bitcast_fusion), channel_id=1, replica_groups=mesh['ctx'=16,'head'=2] {'ctx'}, dimensions={0} | all-to-all | bytes 262144 | tf_op jit(solution)/shard_map/all_to_all | solution.py:403
  16.7 2.0 %route.1 = bf16[16,2,2,2,16,128]{5,4,3,2,1,0:T(8,128)(2,1)} custom-call(s32[16]{0:T(128)} %tile_of_ref.7, bf16[16,2,16,128]{3,2,1,0:T(8,128)(2,1)} %all_to_all.20.held_ref), custom_call_target="tpu_custom_call" | custom-call | tf_op jit(solution)/shard_map/route/pallas_call | solution.py:404
  18.7 2.6 %all-to-all-start.1 = ((bf16[32,2,2,16,128]{4,3,2,1,0:T(8,128)(2,1)}), bf16[32,2,2,16,128]{4,3,2,1,0:T(8,128)(2,1)S(1)}, u32[]{:S(2)}, u32[]{:S(2)}) async-start(bf16[32,2,2,16,128]{4,3,2,1,0:T(8,128)(2,1)} %bitcast.27), calls=%async_computation.1 | async-start | bytes 1048576 | tf_op jit(solution)/shard_map/all_to_all | solution.py:410
  21.3 10.1 %own_forward.1 = (bf16[128,4096]{1,0:T(8,128)(2,1)}, bf16[128,4096]{1,0:T(8,128)(2,1)}, bf16[512,4096]{1,0:T(8,128)(2,1)}, f32[128,4096]{1,0:T(8,128)}, f32[8,4096]{1,0:T(8,128)}) custom-call(s32[1]{0:T(128)} %bitcast.place_ref, s32[16]{0:T(128)} %lengths_ref.3, s32[16]{0:T(128)} %tile_of_ref.7, bf16[4096,128]{1,0:T(8,128)(2,1)} %bitcast.28, ...), custom_call_target="tpu_custom_call" | custom-call | flops 1073741824 | bytes 4194304 | tf_op jit(solution)/shard_map/own_forward/pallas_call | solution.py:418
  31.5 4.8 %all-to-all-done.1.past_ref = bf16[32,2,2,16,128]{4,3,2,1,0:T(8,128)(2,1)S(1)} async-done(((bf16[32,2,2,16,128]{4,3,2,1,0:T(8,128)(2,1)}), bf16[32,2,2,16,128]{4,3,2,1,0:T(8,128)(2,1)S(1)}, u32[]{:S(2)}, u32[]{:S(2)}) %all-to-all-start.1) | async-done | bytes 524320 | tf_op jit(solution)/shard_map/all_to_all | solution.py:410
  36.3 0.0 copy-start.1
  36.3 0.8 copy-done.1
  37.1 10.8 %past.1 = (bf16[4096,128]{1,0:T(8,128)(2,1)}, f32[128,4096]{1,0:T(8,128)}, bf16[32,2,2,16,128]{4,3,2,1,0:T(8,128)(2,1)}, f32[8,4096]{1,0:T(8,128)}) custom-call(s32[1]{0:T(128)} %bitcast.place_ref, s32[16]{0:T(128)} %lengths_ref.3, s32[16]{0:T(128)} %tile_of_ref.7, bf16[4096,128]{1,0:T(8,128)(2,1)} %bitcast.29, bf16[4096,128]{1,0:T(8,128)(2,1)} %bitcast.32, ...), custom_call_target="tpu_custom_call" | custom-call | flops 6442450944 | bytes 4194304 | tf_op jit(solution)/shard_map/past/pallas_call | solution.py:442
  47.9 12.4 %all-to-all-start.2 = ((bf16[32,2,2,16,128]{4,3,2,1,0:T(8,128)(2,1)}), bf16[32,2,2,16,128]{4,3,2,1,0:T(8,128)(2,1)S(1)}, u32[]{:S(2)}, u32[]{:S(2)}) async-start(bf16[32,2,2,16,128]{4,3,2,1,0:T(8,128)(2,1)} %get-tuple-element.25), calls=%async_computation.2 | async-start | bytes 1048576 | tf_op jit(solution)/shard_map/all_to_all | solution.py:504
  60.3 10.7 %own_grads.1 = (bf16[4096,128]{1,0:T(8,128)(2,1)}, bf16[2,512,128]{2,1,0:T(8,128)(2,1)}) custom-call(bf16[4096,128]{1,0:T(8,128)(2,1)} %bitcast.30, bf16[4096,128]{1,0:T(8,128)(2,1)} %bitcast.33, bf16[128,4096]{1,0:T(8,128)(2,1)} %get-tuple-element.16.g_turned_ref, bf16[512,4096]{1,0:T(8,128)(2,1)} %get-tuple-element.20.weight_ref, ...), custom_call_target="tpu_custom_call" | custom-call | flops 2147483648 | bytes 4194304 | tf_op jit(solution)/shard_map/own_grads/pallas_call | solution.py:474
  71.0 1.8 %collective-permute-start = (bf16[2,512,128]{2,1,0:T(8,128)(2,1)}, bf16[2,512,128]{2,1,0:T(8,128)(2,1)S(1)}, u32[]{:S(2)}, u32[]{:S(2)}) collective-permute-start(bf16[2,512,128]{2,1,0:T(8,128)(2,1)} %get-tuple-element.24), channel_id=1, source_target_pairs={{0,1},{1,0},{2,3},{3,2},{4,5},{5,4},{6,7},{7,6},{8,9},{9,8},{10,11... | collective-permute-start | bytes 786440 | tf_op jit(solution)/shard_map/ppermute | solution.py:513
  72.9 2.5 %all-to-all-done.2 = bf16[32,2,2,16,128]{4,3,2,1,0:T(8,128)(2,1)S(1)} async-done(((bf16[32,2,2,16,128]{4,3,2,1,0:T(8,128)(2,1)}), bf16[32,2,2,16,128]{4,3,2,1,0:T(8,128)(2,1)S(1)}, u32[]{:S(2)}, u32[]{:S(2)}) %all-to-all-start.2) | async-done | bytes 524320 | tf_op jit(solution)/shard_map/all_to_all | solution.py:504
  75.3 0.0 copy-start
  75.3 0.8 copy-done
  76.1 2.1 %sum_terms.1 = bf16[16,2,2,16,128]{4,3,2,1,0:T(8,128)(2,1)} custom-call(s32[16]{0:T(128)} %tile_of_ref.7, bf16[16,2,2,2,16,128]{5,4,3,2,1,0:T(8,128)(2,1)} %bitcast.26), custom_call_target="tpu_custom_call" | custom-call | tf_op jit(solution)/shard_map/sum_terms/pallas_call | solution.py:505
  78.2 3.6 %all-to-all-start.3 = ((bf16[32,2,16,128]{3,2,1,0:T(8,128)(2,1)}), bf16[32,2,16,128]{3,2,1,0:T(8,128)(2,1)S(1)}, u32[]{:S(2)}, u32[]{:S(2)}) async-start(bf16[32,2,16,128]{3,2,1,0:T(8,128)(2,1)} %bitcast.34), calls=%async_computation.3 | async-start | bytes 524288 | tf_op jit(solution)/shard_map/all_to_all | solution.py:511
  81.8 0.0 collective-permute-done
  81.8 1.0 %convert_add_fusion = f32[2,512,128]{2,1,0:T(8,128)S(1)} fusion(bf16[2,512,128]{2,1,0:T(8,128)(2,1)S(1)} %collective-permute-done, bf16[2,512,128]{2,1,0:T(8,128)(2,1)} %get-tuple-element.24), kind=kLoop, calls=%fused_computation | loop fusion | flops 393216 | bytes 1048576 | tf_op jit(solution)/shard_map/add | solution.py:514
  82.8 9.7 %all-to-all-done.3 = bf16[32,2,16,128]{3,2,1,0:T(8,128)(2,1)S(1)} async-done(((bf16[32,2,16,128]{3,2,1,0:T(8,128)(2,1)}), bf16[32,2,16,128]{3,2,1,0:T(8,128)(2,1)S(1)}, u32[]{:S(2)}, u32[]{:S(2)}) %all-to-all-start.3) | async-done | bytes 262176 | tf_op jit(solution)/shard_map/all_to_all | solution.py:511
  92.5 0.9 fusion
  (1 shorter events, 0.0 us)
Async XLA Ops:
  18.7 17.6 %all-to-all-start.1 = ((bf16[32,2,2,16,128]{4,3,2,1,0:T(8,128)(2,1)}), bf16[32,2,2,16,128]{4,3,2,1,0:T(8,128)(2,1)S(1)}, u32[]{:S(2)}, u32[]{:S(2)}) async-start(bf16[32,2,2,16,128]{4,3,2,1,0:T(8,128)(2,1)} %bitcast.27), calls=%async_computation.1 | async-start | bytes 1048576 | tf_op jit(solution)/shard_map/all_to_all | solution.py:410
  36.3 0.8 copy-start.1
  47.9 27.4 %all-to-all-start.2 = ((bf16[32,2,2,16,128]{4,3,2,1,0:T(8,128)(2,1)}), bf16[32,2,2,16,128]{4,3,2,1,0:T(8,128)(2,1)S(1)}, u32[]{:S(2)}, u32[]{:S(2)}) async-start(bf16[32,2,2,16,128]{4,3,2,1,0:T(8,128)(2,1)} %get-tuple-element.25), calls=%async_computation.2 | async-start | bytes 1048576 | tf_op jit(solution)/shard_map/all_to_all | solution.py:504
  71.0 10.8 %collective-permute-start = (bf16[2,512,128]{2,1,0:T(8,128)(2,1)}, bf16[2,512,128]{2,1,0:T(8,128)(2,1)S(1)}, u32[]{:S(2)}, u32[]{:S(2)}) collective-permute-start(bf16[2,512,128]{2,1,0:T(8,128)(2,1)} %get-tuple-element.24), channel_id=1, source_target_pairs={{0,1},{1,0},{2,3},{3,2},{4,5},{5,4},{6,7},{7,6},{8,9},{9,8},{10,11... | collective-permute-start | bytes 786440 | tf_op jit(solution)/shard_map/ppermute | solution.py:513
  75.3 0.8 copy-start
  78.2 14.3 %all-to-all-start.3 = ((bf16[32,2,16,128]{3,2,1,0:T(8,128)(2,1)}), bf16[32,2,16,128]{3,2,1,0:T(8,128)(2,1)S(1)}, u32[]{:S(2)}, u32[]{:S(2)}) async-start(bf16[32,2,16,128]{3,2,1,0:T(8,128)(2,1)} %bitcast.34), calls=%async_computation.3 | async-start | bytes 524288 | tf_op jit(solution)/shard_map/all_to_all | solution.py:511
